TPU v7x, 32 devices: a whole 2x2x4 slice. The times are simulated.
32 devices in a mesh: cand: 4 (over x, core), prompt: 4 (over z), tensor: 2 (over y).
Axes of the slice: x: 2, y: 2, z: 4, core: 2. Of those that a mesh axis runs over, the one named last changes fastest.
Arguments:
- owner_index: int32 [4], P('prompt'), may hold values from 0 to 3
- suffix_lengths: int32 [4, 4], P('prompt', 'cand'), may hold values from 64 to 256, as said below
- queries: bfloat16 [4, 1024, 8192], P('prompt', 'cand', 'tensor'), may hold values from -15 to 15
- suffix_kv: bfloat16 [2, 4, 1024, 1024], P(None, 'prompt', 'cand', 'tensor'), may hold values from -6 to 6
- prompt_cache: bfloat16 [2, 4, 4, 4096, 1024], P(None, 'prompt', 'cand', None, 'tensor'), may hold values from -6 to 6
- out_weight: bfloat16 [8192, 4096], P('tensor', 'prompt'), may hold values from -0.09375 to 0.09375
Outputs:
- projected: bfloat16 [4, 1024, 4096], P(None, 'cand', ('prompt', 'tensor'))
Inputs may be any that keep to these rules, and one draw needn't show every extreme that they name: `suffix_lengths`: the first candidate of every prompt has all 256 suffix tokens live.
All inputs are finite; a program needn't handle non-finite values.
Results may differ from a plain program's by a relative error of at most 0.0057.
Values may be sent and summed in bfloat16 or wider, within the bound.
A program may use at most 128 MiB of HBM per device.

v0:
```python
import math

import jax
import jax.numpy as jnp
from jax import lax
from jax.sharding import PartitionSpec as P

HD = 128
SUF = 256


def spread(value, axis, source):
    kept = jnp.where(lax.axis_index(axis) == source, value, 0).astype(value.dtype)
    return lax.psum(kept, axis)


def attend_blocks(query_rows, key_rows, value_rows, length):
    row_count = query_rows.shape[0]
    key_count = key_rows.shape[0]
    kv_count = key_rows.shape[1] // HD
    group_size = query_rows.shape[1] // (kv_count * HD)
    head_step = math.gcd(group_size, max(1, 512 // row_count))
    score_scale = 1.0 / math.sqrt(HD)
    position = jnp.arange(head_step * row_count, dtype=jnp.int32) % row_count
    column = jnp.arange(key_count, dtype=jnp.int32) - (key_count - row_count)
    allowed = (column[None, :] < 0) | (column[None, :] <= position[:, None]) & (
        column[None, :] < length
    )
    pieces = []
    for kv_head in range(kv_count):
        key_head = key_rows[:, kv_head * HD : (kv_head + 1) * HD]
        value_head = value_rows[:, kv_head * HD : (kv_head + 1) * HD]
        query_heads = query_rows[:, kv_head * group_size * HD : (kv_head + 1) * group_size * HD]
        query_heads = query_heads.reshape(row_count, group_size, HD).transpose(1, 0, 2)
        query_heads = query_heads.reshape(group_size // head_step, head_step * row_count, HD)

        def head_block(query_block):
            scores = (
                jnp.einsum("qd,kd->qk", query_block, key_head, preferred_element_type=jnp.float32)
                * score_scale
            )
            scores = jnp.where(allowed, scores, -1e30)
            row_max = jnp.max(scores, axis=-1, keepdims=True)
            exponent = jnp.exp(scores - row_max)
            weights = (exponent / jnp.sum(exponent, axis=-1, keepdims=True)).astype(jnp.bfloat16)
            return jnp.dot(weights, value_head, preferred_element_type=jnp.float32).astype(
                jnp.bfloat16
            )

        finished = lax.map(head_block, query_heads)
        finished = finished.reshape(group_size, row_count, HD).transpose(1, 0, 2)
        pieces.append(finished.reshape(row_count, group_size * HD))
    return jnp.concatenate(pieces, axis=1)


def body(owner_index, suffix_lengths, queries, suffix_kv, prompt_cache, out_weight):
    prompt_slot = spread(prompt_cache[:, 0, 0], "cand", owner_index[0])
    query_rows = queries[0, 0:SUF]
    suffix_part = suffix_kv[:, 0, 0:SUF]
    key_rows = jnp.concatenate([prompt_slot[0], suffix_part[0]], axis=0)
    value_rows = jnp.concatenate([prompt_slot[1], suffix_part[1]], axis=0)
    outputs = attend_blocks(query_rows, key_rows, value_rows, suffix_lengths[0, 0])
    row_count = outputs.shape[0]
    prompt_count = lax.axis_size("prompt")
    tensor_count = lax.axis_size("tensor")
    partial_value = jnp.dot(
        outputs,
        lax.all_gather(out_weight, "prompt", axis=1, tiled=True),
        preferred_element_type=jnp.float32,
    )
    col_count = partial_value.shape[1] // (prompt_count * tensor_count)
    partial_value = partial_value.reshape(row_count, prompt_count, tensor_count, col_count)
    summed = lax.psum_scatter(partial_value, "tensor", scatter_dimension=2, tiled=True).astype(
        jnp.bfloat16
    )
    exchanged = lax.all_to_all(
        summed.reshape(1, row_count, prompt_count, col_count),
        "prompt",
        split_axis=2,
        concat_axis=0,
        tiled=True,
    )
    return exchanged.reshape(prompt_count, row_count, col_count)


def solution(mesh):
    in_specs = (
        P("prompt"),
        P("prompt", "cand"),
        P("prompt", "cand", "tensor"),
        P(None, "prompt", "cand", "tensor"),
        P(None, "prompt", "cand", None, "tensor"),
        P("tensor", "prompt"),
    )
    out_specs = P(None, "cand", ("prompt", "tensor"))
    return jax.shard_map(body, mesh=mesh, in_specs=in_specs, out_specs=out_specs, check_vma=False)
```

profile of v0, /device:TPU:0, one launch (start us, length us, event | category | flops | bytes accessed | tf_op | source)
XLA Modules:
  0.0 712.7 jit_solution(6294872806593082547)
XLA Ops:
  8.0 7.1 fusion.40
  19.6 151.3 %all-reduce.2.cloned.1.call-done = bf16[2,4096,512]{2,1,0:T(8,128)(2,1)} async-done(((bf16[2,4096,512]{2,1,0:T(8,128)(2,1)}), bf16[2,4096,512]{2,1,0:T(8,128)(2,1)}) %all-reduce.2.cloned.1.call-update) | async-done | bytes 8388624 | tf_op jit(solution)/shard_map/psum | solution.py:14
  170.9 3.8 slice_bitcast_fusion
  174.7 5.8 fusion.50
  180.5 29.6 %while.44 = (s32[]{:T(128)}, bf16[4,512,128]{2,1,0:T(8,128)(2,1)S(1)}, bf16[4,512,128]{2,1,0:T(8,128)(2,1)}, bf16[4352,128]{1,0:T(8,128)(2,1)S(1)}, bf16[4352,12...) while((s32[]{:T(128)}, ...), condition=%wide.region_4.5_spmd.clone, body=%wide.region_1.4_spmd.clone.sunk | while | flops 1165425664 | bytes 29268072 | solution.py:50
  180.6 3.7 fusion.96
  184.2 1.4 fusion.97
  185.6 2.4 fusion.98
  188.0 3.6 fusion.96
  193.0 2.4 fusion.98
  195.3 3.6 fusion.96
  200.4 2.4 fusion.98
  202.7 3.6 fusion.96
  207.7 2.4 fusion.98
  211.2 31.6 %while.45 = (s32[]{:T(128)}, bf16[4,512,128]{2,1,0:T(8,128)(2,1)S(1)}, bf16[4,512,128]{2,1,0:T(8,128)(2,1)}, bf16[4352,128]{1,0:T(8,128)(2,1)}, bf16[4352,128]{1...) while((s32[]{:T(128)}, ...), condition=%wide.region_8.9_spmd.clone, body=%wide.region_5.8_spmd.clone.sunk | while | flops 1165425664 | bytes 33724548 | solution.py:50
  211.4 4.2 fusion.101
  217.0 2.4 fusion.103
  219.4 4.1 fusion.101
  224.8 2.4 fusion.103
  227.2 4.1 fusion.101
  232.7 2.4 fusion.103
  235.0 4.1 fusion.101
  240.5 2.4 fusion.103
  244.0 29.6 %while.46 = (s32[]{:T(128)}, bf16[4,512,128]{2,1,0:T(8,128)(2,1)S(1)}, bf16[4,512,128]{2,1,0:T(8,128)(2,1)}, bf16[4352,128]{1,0:T(8,128)(2,1)S(1)}, bf16[4352,12...) while((s32[]{:T(128)}, ...), condition=%wide.region_12.13_spmd.clone, body=%wide.region_9.12_spmd.clone.sunk | while | flops 1165425664 | bytes 29268072 | solution.py:50
  244.0 3.7 fusion.106
  249.0 2.4 fusion.108
  251.4 3.6 fusion.106
  256.4 2.4 fusion.108
  258.8 3.6 fusion.106
  263.8 2.4 fusion.108
  266.2 3.6 fusion.106
  271.2 2.4 fusion.108
  273.9 31.7 %while.47 = (s32[]{:T(128)}, bf16[4,512,128]{2,1,0:T(8,128)(2,1)S(1)}, bf16[4,512,128]{2,1,0:T(8,128)(2,1)}, bf16[4352,128]{1,0:T(8,128)(2,1)}, bf16[4352,128]{1...) while((s32[]{:T(128)}, ...), condition=%wide.region_16.17_spmd.clone, body=%wide.region_13.16_spmd.clone.sunk | while | flops 1165425664 | bytes 33724548 | solution.py:50
  274.1 4.2 fusion.111
  279.6 2.4 fusion.113
  282.0 4.1 fusion.111
  287.4 2.4 fusion.113
  289.8 4.1 fusion.111
  295.3 2.4 fusion.113
  297.7 4.1 fusion.111
  303.2 2.4 fusion.113
  305.8 275.5 %all-gather.2.cloned.1.call-done = bf16[4096,4096]{1,0:T(8,128)(2,1)} async-done(((bf16[4096,1024]{1,0:T(8,128)(2,1)}), bf16[4096,4096]{1,0:T(8,128)(2,1)}) %all-gather.2.cloned.1.call-update) | async-done | bytes 33554448 | tf_op jit(solution)/shard_map/all_gather | solution.py:68
  581.2 25.4 %fusion.41 = f32[256,4096]{1,0:T(8,128)} fusion(bf16[4096,4096]{1,0:T(8,128)(2,1)} %all-gather.2.cloned.1.call-done, bf16[256,1024]{0,1:T(8,128)(2,1)S(1)} %bitcast.151, bf16[256,1024]{0,1:T(8,128)(2,1)S(1)} %bitcast.150, bf16[256,1024]{0,1:T(8,128)(2,1)S(1)} %bitcast.149, bf16[256,1024]{0,1:T(8,128)(2,1)S(1)} %bitcast.148), kind=kOutput, calls=%fused_computation.64 | convolution fusion | flops 8598323200 | bytes 39845888 | tf_op jit(solution)/shard_map/dot_general | solution.py:66
  606.6 6.6 reshape.110
  613.2 6.6 copy.38
  619.8 52.7 %reduce-scatter.2.cloned.1.call-done = f32[256,4,1,512]{3,0,1,2:T(8,128)} async-done(((f32[256,4,2,512]{3,0,1,2:T(8,128)}), f32[256,4,1,512]{3,0,1,2:T(8,128)}) %reduce-scatter.2.cloned.1.call-update) | async-done | bytes 2097168 | tf_op jit(solution)/shard_map/reduce_scatter | solution.py:73
  672.4 1.7 convert_bitcast_fusion
  674.2 30.1 %all_to_all.15 = bf16[1,256,4,512]{3,1,0,2:T(8,128)(2,1)S(1)} all-to-all(bf16[1,256,4,512]{3,1,0,2:T(8,128)(2,1)S(1)} %convert_bitcast_fusion), channel_id=1, replica_groups=mesh['cand'=4,'prompt'=4,'tensor'=2] {'prompt'}, dimensions={2} | all-to-all | bytes 2097152 | tf_op jit(solution)/shard_map/all_to_all | solution.py:76
  (65 shorter events, 27.7 us)
Async XLA Ops:
  7.4 163.5 %all-reduce.2.cloned.1.call-start = ((), (), s32[]{:S(2)}) async-start(), calls=%async_computation.2 | async-start | bytes 16777216 | tf_op jit(solution)/shard_map/psum | solution.py:14
  15.2 1.5 copy-start.7
  15.2 1.8 copy-start.2
  15.2 566.0 %all-gather.2.cloned.1.call-start = ((), (), s32[]{:S(2)}) async-start(), calls=%async_computation.3 | async-start | bytes 41943040 | tf_op jit(solution)/shard_map/all_gather | solution.py:68
  15.8 656.7 %reduce-scatter.2.cloned.1.call-start = ((), (), s32[]{:S(2)}) async-start(), calls=%async_computation.4 | async-start | bytes 6291456 | tf_op jit(solution)/shard_map/reduce_scatter | solution.py:73
  211.2 32.7 %copy-start.4 = (bf16[4352,128]{1,0:T(8,128)(2,1)S(1)}, bf16[4352,128]{1,0:T(8,128)(2,1)}, u32[]{:S(2)}) copy-start(bf16[4352,128]{1,0:T(8,128)(2,1)} %get-tuple-element.609) | copy-start | bytes 3342340
  211.2 32.7 %copy-start.5 = (bf16[4352,128]{1,0:T(8,128)(2,1)S(1)}, bf16[4352,128]{1,0:T(8,128)(2,1)}, u32[]{:S(2)}) copy-start(bf16[4352,128]{1,0:T(8,128)(2,1)} %get-tuple-element.608) | copy-start | bytes 3342340
  215.6 1.4 copy-start.6
  223.4 1.4 copy-start.6
  231.3 1.4 copy-start.6
  239.1 1.4 copy-start.6
  273.8 307.4 %copy-start = (bf16[256,8,128]{0,2,1:T(8,128)(2,1)S(1)}, bf16[256,8,128]{0,2,1:T(8,128)(2,1)}, u32[]{:S(2)}) copy-start(bf16[256,8,128]{0,2,1:T(8,128)(2,1)} %copy.31) | copy-start | bytes 1572868
  273.8 307.4 %copy-start.1 = (bf16[256,8,128]{0,2,1:T(8,128)(2,1)S(1)}, bf16[256,8,128]{0,2,1:T(8,128)(2,1)}, u32[]{:S(2)}) copy-start(bf16[256,8,128]{0,2,1:T(8,128)(2,1)} %copy.33) | copy-start | bytes 1572868
  278.2 1.4 copy-start.3
  286.1 1.4 copy-start.3
  293.9 1.4 copy-start.3
  301.8 1.4 copy-start.3
Sparse Core Ops, SparseCore 0:
  15.3 155.5 all-reduce.1
  619.9 52.4 reduce-scatter.1
Sparse Core Ops, SparseCore 1:
  17.2 563.9 all-gather.1
where the time goes:
time: 713 us
  waiting for transfers between devices  480 us (67%)
  matrix products  125 us (18%)
  other arithmetic  36.4 us (5%)
  blocking collectives  30.1 us (4%)
  local copies, waits for them, and re-layouts  23.6 us (3%)
  between operations  16.5 us (2%)
    all_gather x1, waiting for transfers between devices, body(): lax.all_gather(out_weight, 'prompt', axis=1, tiled=True)  275 us
    psum x1, waiting for transfers between devices, spread(): return lax.psum(kept, axis)  151 us
    dot_general x16, matrix products, head_block(): jnp.einsum('qd,kd->qk', query_block, key_head, preferred_element_type=jnp...  62.1 us
    reduce_scatter x1, waiting for transfers between devices, body(): lax.psum_scatter(partial_value, 'tensor', scatter_dimension=2, tiled=True)  52.7 us
    dot_general x16, matrix products, head_block(): jnp.dot(weights, value_head, preferred_element_type=jnp.float32)  37.8 us
    all_to_all x1, blocking collectives, body(): lax.all_to_all(summed.reshape(1, row_count, prompt_count, col_count), 'pr...  30.1 us
    dot_general x1, matrix products, body(): jnp.dot(outputs, lax.all_gather(out_weight, 'prompt', axis=1, tiled=True)...  25.4 us
    reduce_sum x16, other arithmetic, head_block(): jnp.sum(exponent, axis=-1, keepdims=True)  21.7 us
  transfers between devices with their start and end apart: 3, of which 3 were waited for; matrix products, arithmetic and copies ran while one was open for 19% of the time, Pallas kernels for 0%

commit v1 on v0

v1 whole, which is shorter than its diff:
```python
import functools
import math

import jax
import jax.numpy as jnp
from jax import lax
from jax.experimental import pallas as pl
from jax.experimental.pallas import tpu as pltpu
from jax.sharding import PartitionSpec as P

HD = 128
HEADS_PER_STEP = 2
KEY_CHUNK = 1024


def attend_kernel(length_ref, flip_ref, q_ref, mine_ref, other_ref, sk_ref, sv_ref, o_ref, k_buf, v_buf, bias_buf):
    plen = mine_ref.shape[0]
    suf = sk_ref.shape[0]

    @pl.when(pl.program_id(0) == 0)
    def _():
        flip = flip_ref[0] != 0

        @pl.when(flip)
        def _():
            k_buf[0:plen, :] = other_ref[...]
            v_buf[0:plen, 0:HD] = mine_ref[...]

        @pl.when(jnp.logical_not(flip))
        def _():
            k_buf[0:plen, :] = mine_ref[...]
            v_buf[0:plen, 0:HD] = other_ref[...]

        k_buf[plen:, :] = sk_ref[...]
        v_buf[plen:, 0:HD] = sv_ref[...]
        v_buf[:, HD:] = jnp.ones((plen + suf, HD), jnp.bfloat16)
        row = lax.broadcasted_iota(jnp.int32, (suf, suf), 0)
        col = lax.broadcasted_iota(jnp.int32, (suf, suf), 1)
        allowed = (col <= row) & (col < length_ref[0])
        bias_buf[...] = jnp.where(allowed, 0.0, -1e30)

    scale = math.log2(math.e) / math.sqrt(HD)
    chunks = [(s, KEY_CHUNK) for s in range(0, plen, KEY_CHUNK)] + [(plen, suf)]
    for head in range(q_ref.shape[1] // HD):
        q = q_ref[:, head * HD : (head + 1) * HD]
        scores = []
        for start, size in chunks:
            s = lax.dot_general(
                q, k_buf[start : start + size, :], (((1,), (1,)), ((), ())), preferred_element_type=jnp.float32
            )
            if start == plen:
                s = s + bias_buf[...]
            scores.append(s)
        top = functools.reduce(jnp.maximum, [jnp.max(s, axis=1, keepdims=True) for s in scores])
        shift = top * scale
        total = None
        for (start, size), s in zip(chunks, scores):
            p = jnp.exp2(s * scale - shift).astype(jnp.bfloat16)
            part = jnp.dot(p, v_buf[start : start + size, :], preferred_element_type=jnp.float32)
            total = part if total is None else total + part
        o_ref[:, head * HD : (head + 1) * HD] = (total[:, 0:HD] / total[:, HD:]).astype(jnp.bfloat16)


def attend_head(head, length, flip, queries, mine, other, suffix_k, suffix_v, group):
    rows = queries.shape[0]
    suf = suffix_k.shape[0]
    plen = mine.shape[0]
    steps = group // HEADS_PER_STEP
    width = HEADS_PER_STEP * HD
    keys = plen + suf
    return pl.pallas_call(
        attend_kernel,
        grid=(steps,),
        out_shape=jax.ShapeDtypeStruct((rows, group * HD), jnp.bfloat16),
        in_specs=[
            pl.BlockSpec(memory_space=pltpu.SMEM),
            pl.BlockSpec(memory_space=pltpu.SMEM),
            pl.BlockSpec((rows, width), lambda i: (0, head * steps + i)),
            pl.BlockSpec((plen, HD), lambda i: (0, 0)),
            pl.BlockSpec((plen, HD), lambda i: (0, 0)),
            pl.BlockSpec((suf, HD), lambda i: (0, head)),
            pl.BlockSpec((suf, HD), lambda i: (0, head)),
        ],
        out_specs=pl.BlockSpec((rows, width), lambda i: (0, i)),
        scratch_shapes=[
            pltpu.VMEM((keys, HD), jnp.bfloat16),
            pltpu.VMEM((keys, 2 * HD), jnp.bfloat16),
            pltpu.VMEM((suf, suf), jnp.float32),
        ],
        compiler_params=pltpu.CompilerParams(vmem_limit_bytes=48 * 1024 * 1024),
        cost_estimate=pl.CostEstimate(
            flops=16 * group * rows * keys * HD, bytes_accessed=4 * keys * HD, transcendentals=group * rows * keys
        ),
    )(length, flip, queries, mine, other, suffix_k, suffix_v)


def flip_perm(count, bit):
    return [(i, i ^ bit) for i in range(count)]


def body(owner_index, suffix_lengths, queries, suffix_kv, prompt_cache, out_weight):
    cand_count = lax.axis_size("cand")
    prompt_count = lax.axis_size("prompt")
    tensor_count = lax.axis_size("tensor")
    owner = owner_index[0]
    me = lax.axis_index("cand")
    side = me % 2
    rows = queries.shape[1]
    kv_count = suffix_kv.shape[3] // HD
    group = queries.shape[2] // (kv_count * HD)

    cache = prompt_cache[:, 0, 0]
    keep = lax.dynamic_index_in_dim(cache, side, 0, keepdims=False)
    give = lax.dynamic_index_in_dim(cache, 1 - side, 0, keepdims=False)

    def same(bit):
        return (owner & bit) == (me & bit)

    pairs = []
    for head in range(kv_count):
        cols = slice(head * HD, (head + 1) * HD)
        got = lax.ppermute(give[:, cols], "cand", flip_perm(cand_count, 1))
        part = jnp.where(same(1), keep[:, cols], got)
        bit = 2
        while bit < cand_count:
            got = lax.ppermute(part, "cand", flip_perm(cand_count, bit))
            part = jnp.where(same(bit), part, got)
            bit *= 2
        pairs.append((part, lax.ppermute(part, "cand", flip_perm(cand_count, 1))))

    length = suffix_lengths.reshape(1)
    flip = side.reshape(1).astype(jnp.int32)
    query_rows = queries[0]
    gathered = []
    for head in range(kv_count):
        mine, other = pairs[head]
        done = attend_head(
            head, length, flip, query_rows, mine, other, suffix_kv[0, 0], suffix_kv[1, 0], group
        )
        gathered.append(lax.all_gather(done, "prompt", axis=0, tiled=True))

    def project(weight):
        total = None
        for head in range(kv_count):
            piece = weight[head * group * HD : (head + 1) * group * HD]
            part = jnp.dot(gathered[head], piece, preferred_element_type=jnp.float32)
            total = part if total is None else total + part
        return total

    col_count = out_weight.shape[1] // tensor_count
    if tensor_count == 2:
        here = lax.axis_index("tensor")
        theirs = lax.dynamic_slice_in_dim(out_weight, (1 - here) * col_count, col_count, 1)
        ours = lax.dynamic_slice_in_dim(out_weight, here * col_count, col_count, 1)
        sent = project(theirs).astype(jnp.bfloat16)
        arrived = lax.ppermute(sent, "tensor", flip_perm(2, 1))
        result = (project(ours) + arrived.astype(jnp.float32)).astype(jnp.bfloat16)
    else:
        total = project(out_weight)
        result = lax.psum_scatter(total, "tensor", scatter_dimension=1, tiled=True).astype(jnp.bfloat16)
    return result.reshape(prompt_count, rows, col_count)


def solution(mesh):
    in_specs = (
        P("prompt"),
        P("prompt", "cand"),
        P("prompt", "cand", "tensor"),
        P(None, "prompt", "cand", "tensor"),
        P(None, "prompt", "cand", None, "tensor"),
        P("tensor", "prompt"),
    )
    out_specs = P(None, "cand", ("prompt", "tensor"))
    return jax.shard_map(body, mesh=mesh, in_specs=in_specs, out_specs=out_specs, check_vma=False)
```

time: 713 us -> 305 us (0.43)
  waiting for transfers between devices: 480 us -> 146 us
  matrix products: 125 us -> 26.8 us
  Pallas kernels: 0 us -> 87.2 us
  blocking collectives: 30.1 us -> 0 us
  other arithmetic: 36.4 us -> 12.1 us
  local copies, waits for them, and re-layouts: 23.6 us -> 10.5 us
  starting transfers between devices: 0.09 us -> 8.01 us
    all_gather x1 -> x4, waiting for transfers between devices: 275 us -> 91.1 us  [body(): gathered.append(lax.all_gather(done, 'prompt', axis=0, tiled=True))]
    psum x1 -> x0, waiting for transfers between devices: 151 us -> none  [spread(): return lax.psum(kept, axis)]
    dot_general x33 -> x8, matrix products: 125 us -> 26.8 us  [project(): part = jnp.dot(gathered[head], piece, preferred_element_type=jnp.float32)]
    pallas_call x0 -> x4, Pallas kernels: none -> 87.2 us  [attend_head(): pl.pallas_call(attend_kernel, grid=(steps,), out_shape=jax.ShapeDtypeStru...]
    ppermute x0 -> x13, waiting for transfers between devices: none -> 54.4 us  [the longest x4 28.4 us: body(): got = lax.ppermute(part, 'cand', flip_perm(cand_count, bit))]
    reduce_scatter x1 -> x0, waiting for transfers between devices: 52.7 us -> none  [body(): lax.psum_scatter(partial_value, 'tensor', scatter_dimension=2, tiled=True)]
    all_to_all x1 -> x0, blocking collectives: 30.1 us -> none  [body(): lax.all_to_all(summed.reshape(1, row_count, prompt_count, col_count), 'pr...]
    reduce_sum x16 -> x0, other arithmetic: 21.7 us -> none  [head_block(): jnp.sum(exponent, axis=-1, keepdims=True)]
  transfers between devices with their start and end apart: 3 -> 17, of which waited for: 3 -> 15; matrix products, arithmetic and copies ran while one was open for 19% -> 9% of each run, Pallas kernels for 0% -> 29%
where the time goes in v1:
time: 305 us
  waiting for transfers between devices  146 us (48%)
  Pallas kernels  87.2 us (29%)
  matrix products  26.8 us (9%)
  between operations  14.6 us (5%)
  other arithmetic  12.1 us (4%)
  local copies, waits for them, and re-layouts  10.5 us (3%)
  starting transfers between devices  8.01 us (3%)
    all_gather x4, waiting for transfers between devices, body(): gathered.append(lax.all_gather(done, 'prompt', axis=0, tiled=True))  91.1 us
    pallas_call x4, Pallas kernels, attend_head(): pl.pallas_call(attend_kernel, grid=(steps,), out_shape=jax.ShapeDtypeStru...  87.2 us
    ppermute x4, waiting for transfers between devices, body(): got = lax.ppermute(part, 'cand', flip_perm(cand_count, bit))  28.4 us
    dot_general x8, matrix products, project(): part = jnp.dot(gathered[head], piece, preferred_element_type=jnp.float32)  26.8 us
    ppermute x1, waiting for transfers between devices, body(): arrived = lax.ppermute(sent, 'tensor', flip_perm(2, 1))  13.2 us
    ppermute x4, waiting for transfers between devices, body(): pairs.append((part, lax.ppermute(part, 'cand', flip_perm(cand_count, 1))))  7.09 us
  transfers between devices with their start and end apart: 17, of which 15 were waited for; matrix products, arithmetic and copies ran while one was open for 9% of the time, Pallas kernels for 29%

profile of v1, /device:TPU:0, one launch (start us, length us, event | category | flops | bytes accessed | tf_op | source)
XLA Modules:
  0.0 304.8 jit_solution(18107385470100106553)
XLA Ops:
  6.5 6.0 %dynamic-slice_bitcast_fusion.1 = (bf16[4096,512]{1,0:T(8,128)(2,1)}, bf16[4096,512]{1,0:T(8,128)(2,1)S(1)}) fusion(bf16[2,1,1,4096,512]{4,3,2,1,0:T(8,128)(2,1)} %param.10, s32[]{:T(128)S(6)} %select_n.61, s32[]{:T(128)S(6)} %select_n.62), kind=kLoop, calls=%fused_computation.1 | loop fusion | bytes 16777224 | tf_op jit(solution)/shard_map/jit(dynamic_index_in_dim)/squeeze | solution.py:113
  12.5 2.5 fusion.20
  15.0 0.5 collective-permute-start.9
  15.5 0.5 collective-permute-start.3
  16.7 1.3 collective-permute-done.9
  17.9 3.0 collective-permute-done.6
  20.9 1.5 collective-permute-done.3
  22.4 1.0 copy-done.2
  23.4 4.7 %slice_select_fusion = (bf16[4096,128]{1,0:T(8,128)(2,1)}, bf16[4096,128]{1,0:T(8,128)(2,1)}, bf16[4096,128]{1,0:T(8,128)(2,1)}, bf16[4096,128]{1,0:T(8,128)(2,1)S(1)}) fusion(bf16[4096,128]{1,0:T(8,128)(2,1)S(1)} %collective-permute-done.9, bf16[4096,512]{1,0:T(8,128)(2,1)} %get-tuple-element.5, pred[]{:T(512)S(6)} %eq.7, ...), kind=kLoop, calls=%fused_computation.14 | loop fusion | flops 2097152 | bytes 12582913 | tf_op jit(solution)/shard_map/jit(_where)/select_n | solution.py:123
  28.1 2.9 collective-permute-start.1
  30.9 22.9 %collective-permute-done.1 = bf16[4096,128]{1,0:T(8,128)(2,1)} collective-permute-done((bf16[4096,128]{1,0:T(8,128)(2,1)S(1)}, bf16[4096,128]{1,0:T(8,128)(2,1)}, u32[]{:S(2)}, u32[]{:S(2)}) %collective-permute-start.1) | collective-permute-done | bytes 1048608 | tf_op jit(solution)/shard_map/ppermute | solution.py:126
  53.9 1.3 broadcast_select_fusion.3.mine_ref
  55.2 0.1 collective-permute-start.2
  55.9 1.1 slice_bitcast_fusion
  57.0 0.6 collective-permute-start.4
  57.6 0.3 collective-permute-done.2.other_ref
  57.9 21.8 %shard_map.64 = bf16[256,1024]{1,0:T(8,128)(2,1)} custom-call(s32[1]{0:T(128)} %bitcast.22.length_ref, s32[1]{0:T(128)} %bitcast.1.flip_ref, bf16[256,4096]{1,0:T(8,128)(2,1)S(1)} %bitcast.26, bf16[4096,128]{1,0:T(8,128)(2,1)S(1)} %broadcast_select_fusion.3.mine_ref, bf16[4096,128]{1,0:T(8,128)(2,1)S(1)} %collective-permute-done.2.other_ref, ...), custom_call_target="tpu_custom_call" | custom-call | flops 18253611008 | bytes 2228224 | tf_op jit(solution)/shard_map/pallas_call | solution.py:71
  79.7 0.2 all-gather.7.cloned.1.call-start
  80.0 3.0 collective-permute-done.4
  82.9 1.3 broadcast_select_fusion.2.mine_ref
  84.4 0.6 collective-permute-start.7
  84.9 2.1 collective-permute-done.5.other_ref
  87.0 21.8 %shard_map.65 = bf16[256,1024]{1,0:T(8,128)(2,1)} custom-call(s32[1]{0:T(128)} %bitcast.23.length_ref, s32[1]{0:T(128)} %bitcast.1.flip_ref, bf16[256,4096]{1,0:T(8,128)(2,1)S(1)} %bitcast.27, bf16[4096,128]{1,0:T(8,128)(2,1)S(1)} %broadcast_select_fusion.2.mine_ref, bf16[4096,128]{1,0:T(8,128)(2,1)S(1)} %collective-permute-done.5.other_ref, ...), custom_call_target="tpu_custom_call" | custom-call | flops 18253611008 | bytes 2228224 | tf_op jit(solution)/shard_map/pallas_call | solution.py:71
  108.9 1.4 collective-permute-done.7
  110.2 1.3 broadcast_select_fusion.1.mine_ref
  111.6 0.1 collective-permute-start.8
  111.7 0.6 collective-permute-start.10
  112.3 2.0 collective-permute-done.8.other_ref
  114.3 21.8 %shard_map.66 = bf16[256,1024]{1,0:T(8,128)(2,1)} custom-call(s32[1]{0:T(128)} %bitcast.24.length_ref, s32[1]{0:T(128)} %bitcast.1.flip_ref, bf16[256,4096]{1,0:T(8,128)(2,1)S(1)} %bitcast.28, bf16[4096,128]{1,0:T(8,128)(2,1)S(1)} %broadcast_select_fusion.1.mine_ref, bf16[4096,128]{1,0:T(8,128)(2,1)S(1)} %collective-permute-done.8.other_ref, ...), custom_call_target="tpu_custom_call" | custom-call | flops 18253611008 | bytes 2228224 | tf_op jit(solution)/shard_map/pallas_call | solution.py:71
  136.1 0.3 all-gather.11.cloned.1.call-start
  136.4 1.1 collective-permute-done.10
  137.6 1.3 broadcast_select_fusion.mine_ref
  139.0 2.6 collective-permute-done.11.other_ref
  141.6 21.8 %shard_map.67 = bf16[256,1024]{1,0:T(8,128)(2,1)} custom-call(s32[1]{0:T(128)} %bitcast.25.length_ref, s32[1]{0:T(128)} %bitcast.1.flip_ref, bf16[256,4096]{1,0:T(8,128)(2,1)S(1)} %bitcast.29, bf16[4096,128]{1,0:T(8,128)(2,1)S(1)} %broadcast_select_fusion.mine_ref, bf16[4096,128]{1,0:T(8,128)(2,1)S(1)} %collective-permute-done.11.other_ref, ...), custom_call_target="tpu_custom_call" | custom-call | flops 18253611008 | bytes 2228224 | tf_op jit(solution)/shard_map/pallas_call | solution.py:71
  163.5 3.1 %fusion.8 = f32[1024,512]{1,0:T(8,128)S(1)} fusion(bf16[1024,1024]{1,0:T(8,128)(2,1)} %all-gather.5.cloned.1.call-done, bf16[4096,1024]{1,0:T(8,128)(2,1)} %param.11, s32[]{:T(128)S(6)} %select_n.72), kind=kOutput, calls=%fused_computation.10 | convolution fusion | flops 1073741824 | bytes 5242884 | tf_op jit(solution)/shard_map/dot_general | solution.py:146
  166.6 7.6 %all-gather.7.cloned.1.call-done = bf16[1024,1024]{1,0:T(8,128)(2,1)} async-done(((bf16[256,1024]{1,0:T(8,128)(2,1)}), bf16[1024,1024]{1,0:T(8,128)(2,1)}) %all-gather.7.cloned.1.call-update) | async-done | bytes 2097168 | tf_op jit(solution)/shard_map/all_gather | solution.py:140
  174.2 4.5 %fusion.6 = f32[1024,512]{1,0:T(8,128)} fusion(bf16[1024,1024]{1,0:T(8,128)(2,1)} %all-gather.7.cloned.1.call-done, bf16[4096,1024]{1,0:T(8,128)(2,1)} %param.11, s32[]{:T(128)S(6)} %add.51, s32[]{:T(128)S(6)} %select_n.72), kind=kOutput, calls=%fused_computation.8 | convolution fusion | flops 1073741824 | bytes 5242888 | tf_op jit(solution)/shard_map/dot_general | solution.py:146
  178.7 41.8 %all-gather.9.cloned.1.call-done = bf16[1024,1024]{1,0:T(8,128)(2,1)} async-done(((bf16[256,1024]{1,0:T(8,128)(2,1)}), bf16[1024,1024]{1,0:T(8,128)(2,1)}) %all-gather.9.cloned.1.call-update) | async-done | bytes 2097168 | tf_op jit(solution)/shard_map/all_gather | solution.py:140
  220.5 4.5 %fusion.4 = f32[1024,512]{1,0:T(8,128)} fusion(bf16[1024,1024]{1,0:T(8,128)(2,1)} %all-gather.9.cloned.1.call-done, bf16[4096,1024]{1,0:T(8,128)(2,1)} %param.11, s32[]{:T(128)S(6)} %add.52, s32[]{:T(128)S(6)} %select_n.72), kind=kOutput, calls=%fused_computation.6 | convolution fusion | flops 1073741824 | bytes 5242888 | tf_op jit(solution)/shard_map/dot_general | solution.py:146
  224.9 41.7 %all-gather.11.cloned.1.call-done = bf16[1024,1024]{1,0:T(8,128)(2,1)} async-done(((bf16[256,1024]{1,0:T(8,128)(2,1)}), bf16[1024,1024]{1,0:T(8,128)(2,1)}) %all-gather.11.cloned.1.call-update) | async-done | bytes 2097168 | tf_op jit(solution)/shard_map/all_gather | solution.py:140
  266.6 4.6 %add_convert_fusion.1 = bf16[1024,512]{1,0:T(8,128)(2,1)S(1)} fusion(f32[1024,512]{1,0:T(8,128)} %fusion.4, f32[1024,512]{1,0:T(8,128)S(1)} %fusion.8, f32[1024,512]{1,0:T(8,128)} %fusion.6, bf16[1024,1024]{1,0:T(8,128)(2,1)} %all-gather.11.cloned.1.call-done, bf16[4096,1024]{1,0:T(8,128)(2,1)} %param.11, s32[]{:T(128)S(6)} %add.53, s32[]{:T(128)S(6)} %select_n.72), kind=kOutput, calls=%fused_computation.3 | convolution fusion | flops 1075838976 | bytes 10485768 | tf_op jit(solution)/shard_map/dot_general | solution.py:146
  271.2 1.5 collective-permute-start.12
  272.7 2.5 fusion.16
  275.2 2.6 fusion.14
  277.9 2.6 fusion.10
  280.5 2.5 fusion.12
  283.0 13.2 %collective-permute-done.12 = bf16[1024,512]{1,0:T(8,128)(2,1)S(1)} collective-permute-done((bf16[1024,512]{1,0:T(8,128)(2,1)S(1)}, bf16[1024,512]{1,0:T(8,128)(2,1)S(1)}, u32[]{:S(2)}, u32[]{:S(2)}) %collective-permute-start.12) | collective-permute-done | bytes 1048608 | tf_op jit(solution)/shard_map/ppermute | solution.py:156
  296.2 2.1 add_convert_fusion
  (23 shorter events, 0.4 us)
Async XLA Ops:
  6.5 156.9 %all-gather.5.cloned.1.call-start = ((), (), s32[]{:S(2)}) async-start(), calls=%async_computation | async-start | bytes 2621440 | tf_op jit(solution)/shard_map/all_gather | solution.py:140
  15.0 3.0 collective-permute-start.9
  15.4 5.5 %collective-permute-start.6 = (bf16[4096,128]{1,0:T(8,128)(2,1)}, bf16[4096,128]{1,0:T(8,128)(2,1)S(1)}, u32[]{:S(2)}, u32[]{:S(2)}) collective-permute-start(bf16[4096,128]{1,0:T(8,128)(2,1)} %get-tuple-element.12), channel_id=1, source_target_pairs={{0,8},{8,0},{16,24},{24,16},{1,9},{9,1},{17,25},{25,17},{2,10},{10... | collective-permute-start | bytes 3145736 | tf_op jit(solution)/shard_map/ppermute | solution.py:122
  15.5 6.9 %collective-permute-start.3 = (bf16[4096,128]{1,0:T(8,128)(2,1)}, bf16[4096,128]{1,0:T(8,128)(2,1)S(1)}, u32[]{:S(2)}, u32[]{:S(2)}) collective-permute-start(bf16[4096,128]{1,0:T(8,128)(2,1)} %get-tuple-element.13), channel_id=1, source_target_pairs={{0,8},{8,0},{16,24},{24,16},{1,9},{9,1},{17,25},{25,17},{2,10},{10... | collective-permute-start | bytes 3145736 | tf_op jit(solution)/shard_map/ppermute | solution.py:122
  16.0 6.5 %collective-permute-start = (bf16[4096,128]{1,0:T(8,128)(2,1)}, bf16[4096,128]{1,0:T(8,128)(2,1)}, u32[]{:S(2)}, u32[]{:S(2)}) collective-permute-start(bf16[4096,128]{1,0:T(8,128)(2,1)} %get-tuple-element.14), channel_id=1, source_target_pairs={{0,8},{8,0},{16,24},{24,16},{1,9},{9,1},{17,25},{25,17},{2,10},{10... | collective-permute-start | bytes 3145736 | tf_op jit(solution)/shard_map/ppermute | solution.py:122
  22.4 1.0 copy-start.2
  28.1 25.8 %collective-permute-start.1 = (bf16[4096,128]{1,0:T(8,128)(2,1)S(1)}, bf16[4096,128]{1,0:T(8,128)(2,1)}, u32[]{:S(2)}, u32[]{:S(2)}) collective-permute-start(bf16[4096,128]{1,0:T(8,128)(2,1)S(1)} %get-tuple-element.10), channel_id=1, source_target_pairs={{0,16},{8,24},{16,0},{24,8},{1,17},{9,25},{17,1},{25,9},{2,18},{10... | collective-permute-start | bytes 3145736 | tf_op jit(solution)/shard_map/ppermute | solution.py:126
  30.9 27.0 %copy-start = (bf16[1,256,4096]{2,1,0:T(8,128)(2,1)S(1)}, bf16[1,256,4096]{2,1,0:T(8,128)(2,1)}, u32[]{:S(2)}) copy-start(bf16[1,256,4096]{2,1,0:T(8,128)(2,1)} %param.8) | copy-start | bytes 6291460
  55.2 2.7 collective-permute-start.2
  57.0 25.9 %collective-permute-start.4 = (bf16[4096,128]{1,0:T(8,128)(2,1)}, bf16[4096,128]{1,0:T(8,128)(2,1)}, u32[]{:S(2)}, u32[]{:S(2)}) collective-permute-start(bf16[4096,128]{1,0:T(8,128)(2,1)} %get-tuple-element.9), channel_id=1, source_target_pairs={{0,16},{8,24},{16,0},{24,8},{1,17},{9,25},{17,1},{25,9},{2,18},{10... | collective-permute-start | bytes 3145736 | tf_op jit(solution)/shard_map/ppermute | solution.py:126
  79.7 94.5 %all-gather.7.cloned.1.call-start = ((), (), s32[]{:S(2)}) async-start(), calls=%async_computation.1 | async-start | bytes 2621440 | tf_op jit(solution)/shard_map/all_gather | solution.py:140
  84.3 2.7 collective-permute-start.5
  84.4 25.9 %collective-permute-start.7 = (bf16[4096,128]{1,0:T(8,128)(2,1)}, bf16[4096,128]{1,0:T(8,128)(2,1)}, u32[]{:S(2)}, u32[]{:S(2)}) collective-permute-start(bf16[4096,128]{1,0:T(8,128)(2,1)} %get-tuple-element.8), channel_id=1, source_target_pairs={{0,16},{8,24},{16,0},{24,8},{1,17},{9,25},{17,1},{25,9},{2,18},{10... | collective-permute-start | bytes 3145736 | tf_op jit(solution)/shard_map/ppermute | solution.py:126
  108.8 111.7 %all-gather.9.cloned.1.call-start = ((), (), s32[]{:S(2)}) async-start(), calls=%async_computation.2 | async-start | bytes 2621440 | tf_op jit(solution)/shard_map/all_gather | solution.py:140
  111.6 2.7 collective-permute-start.8
  111.7 25.9 %collective-permute-start.10 = (bf16[4096,128]{1,0:T(8,128)(2,1)}, bf16[4096,128]{1,0:T(8,128)(2,1)}, u32[]{:S(2)}, u32[]{:S(2)}) collective-permute-start(bf16[4096,128]{1,0:T(8,128)(2,1)} %get-tuple-element.7), channel_id=1, source_target_pairs={{0,16},{8,24},{16,0},{24,8},{1,17},{9,25},{17,1},{25,9},{2,18},{10... | collective-permute-start | bytes 3145736 | tf_op jit(solution)/shard_map/ppermute | solution.py:126
  136.1 130.5 %all-gather.11.cloned.1.call-start = ((), (), s32[]{:S(2)}) async-start(), calls=%async_computation.3 | async-start | bytes 2621440 | tf_op jit(solution)/shard_map/all_gather | solution.py:140
  138.9 2.7 collective-permute-start.11
  266.6 6.1 %copy-start.3 = (bf16[1024,1024]{1,0:T(8,128)(2,1)S(1)}, bf16[1024,1024]{1,0:T(8,128)(2,1)}, u32[]{:S(2)}) copy-start(bf16[1024,1024]{1,0:T(8,128)(2,1)} %all-gather.5.cloned.1.call-done) | copy-start | bytes 6291460
  271.2 4.0 %copy-start.4 = (bf16[1024,1024]{1,0:T(8,128)(2,1)S(1)}, bf16[1024,1024]{1,0:T(8,128)(2,1)}, u32[]{:S(2)}) copy-start(bf16[1024,1024]{1,0:T(8,128)(2,1)} %all-gather.7.cloned.1.call-done) | copy-start | bytes 6291460
  271.2 25.0 %collective-permute-start.12 = (bf16[1024,512]{1,0:T(8,128)(2,1)S(1)}, bf16[1024,512]{1,0:T(8,128)(2,1)S(1)}, u32[]{:S(2)}, u32[]{:S(2)}) collective-permute-start(bf16[1024,512]{1,0:T(8,128)(2,1)S(1)} %add_convert_fusion.1), channel_id=1, source_target_pairs={{0,1},{1,0},{2,3},{3,2},{4,5},{5,4},{6,7},{7,6},{8,9},{9,8},{10,11... | collective-permute-start | bytes 3145736 | tf_op jit(solution)/shard_map/ppermute | solution.py:156
  275.2 2.6 copy-start.1
  277.9 2.6 copy-start.5
Sparse Core Ops, SparseCore 0:
  79.9 48.0 all-gather.4
  129.5 44.6 all-gather.6
  175.8 44.6 all-gather.8
  221.9 44.6 all-gather.10

commit v2 on v1

--- a/solution.py
+++ b/solution.py
@@ -98,10 +98,313 @@
     return [(i, i ^ bit) for i in range(count)]
 
 
+def fused_kernel(
+    owner_ref, length_ref, q_ref, suf_ref, cache_ref, w_ref, out_ref,
+    keep, got, xgot, other, k_buf, v_buf, bias_buf, att, w_buf, acc, y_send, y_recv,
+    keep_sem, core_send, core_recv, x_send, x_recv, swap_send, swap_recv,
+    left_send, right_send, z_recv, y_send_sem, y_recv_sem, w_sem,
+):
+    heads, plen, _ = keep.shape
+    prompts, units, rows, width = att.shape
+    suf = suf_ref.shape[1]
+    me = lax.axis_index("cand")
+    z = lax.axis_index("prompt")
+    here = lax.axis_index("tensor")
+    side = lax.rem(me, 2)
+    core = {"cand": me + 1 - 2 * side}
+    across = {"cand": lax.rem(me + 2, 4)}
+    beside = {"tensor": 1 - here}
+    left = {"prompt": z - 1}
+    right = {"prompt": z + 1}
+    mesh_id = pl.DeviceIdType.MESH
+    has_left = z > 0
+    has_right = z < prompts - 1
+
+    barrier = pltpu.get_barrier_semaphore()
+    for device in (core, across, beside):
+        pl.semaphore_signal(barrier, inc=1, device_id=device, device_id_type=mesh_id)
+
+    @pl.when(has_left)
+    def _():
+        pl.semaphore_signal(barrier, inc=1, device_id=left, device_id_type=mesh_id)
+
+    @pl.when(has_right)
+    def _():
+        pl.semaphore_signal(barrier, inc=1, device_id=right, device_id_type=mesh_id)
+
+    pl.semaphore_wait(barrier, 3 + has_left.astype(jnp.int32) + has_right.astype(jnp.int32))
+
+    def remote(src, dst, send, recv, device):
+        return pltpu.make_async_remote_copy(
+            src_ref=src, dst_ref=dst, send_sem=send, recv_sem=recv, device_id=device, device_id_type=mesh_id
+        )
+
+    def keep_copy(h):
+        return pltpu.make_async_copy(cache_ref.at[side, :, pl.ds(h * HD, HD)], keep.at[h], keep_sem.at[h])
+
+    def core_copy(h):
+        return remote(
+            cache_ref.at[1 - side, :, pl.ds(h * HD, HD)], got.at[h], core_send.at[h], core_recv.at[h], core
+        )
+
+    def x_copy(h):
+        return remote(keep.at[h], xgot.at[h], x_send.at[h], x_recv.at[h], across)
+
+    def swap_copy(h):
+        return remote(got.at[h], other.at[h], swap_send.at[h], swap_recv.at[h], core)
+
+    def left_copy(p, u):
+        return remote(att.at[p, u], att.at[p, u], left_send.at[p, u], z_recv.at[p, u], left)
+
+    def right_copy(p, u):
+        return remote(att.at[p, u], att.at[p, u], right_send.at[p, u], z_recv.at[p, u], right)
+
+    def w_copy():
+        return pltpu.make_async_copy(w_ref, w_buf, w_sem)
+
+    owner = owner_ref[0]
+    same_core = lax.rem(owner, 2) == side
+    same_chip = lax.div(owner, 2) == lax.div(me, 2)
+
+    for h in range(heads):
+        core_copy(h).start()
+        keep_copy(h).start()
+    w_copy().start()
+
+    v_buf[:, HD:] = jnp.ones((plen + suf, HD), jnp.bfloat16)
+    row = lax.broadcasted_iota(jnp.int32, (suf, suf), 0)
+    col = lax.broadcasted_iota(jnp.int32, (suf, suf), 1)
+    bias_buf[...] = jnp.where((col <= row) & (col < length_ref[0]), 0.0, -1e30)
+
+    def first(h, carry):
+        keep_copy(h).wait()
+        core_copy(h).wait_recv()
+        keep[h] = jnp.where(same_core, keep[h], got[h])
+
+        @pl.when(h == 0)
+        def _():
+            x_copy(h).start()
+
+        return carry
+
+    lax.fori_loop(0, heads, first, 0)
+
+    def prepare(h):
+        x_copy(h).wait_recv()
+
+        @pl.when(h + 1 < heads)
+        def _():
+            x_copy(h + 1).start()
+
+        got[h] = jnp.where(same_chip, keep[h], xgot[h])
+        swap_copy(h).start()
+
+    prepare(0)
+    acc[...] = jnp.zeros_like(acc)
+    w_copy().wait()
+
+    def in_range(u):
+        return (u >= 0) & (u < units)
+
+    def project(u):
+        def block(p, carry):
+            acc[p] += jnp.dot(
+                att[p, u], w_buf[pl.ds(pl.multiple_of(u * width, width), width), :],
+                preferred_element_type=jnp.float32,
+            )
+            return carry
+
+        lax.fori_loop(0, prompts, block, 0)
+
+    def pieces(u):
+        @pl.when((u < units) & has_left)
+        def _():
+            left_copy(z, u).start()
+
+        @pl.when((u < units) & has_right)
+        def _():
+            right_copy(z, u).start()
+
+        for hop in range(1, prompts):
+            late = u - hop
+
+            @pl.when(in_range(late) & (z >= hop))
+            def _():
+                right_copy(z - hop, late).wait_recv()
+
+                @pl.when(has_right)
+                def _():
+                    right_copy(z - hop, late).start()
+
+            @pl.when(in_range(late) & (z + hop < prompts))
+            def _():
+                left_copy(z + hop, late).wait_recv()
+
+                @pl.when(has_left)
+                def _():
+                    left_copy(z + hop, late).start()
+
+        @pl.when(in_range(u - prompts + 1))
+        def _():
+            project(u - prompts + 1)
+
+    scale = math.log2(math.e) / math.sqrt(HD)
+    chunks = [(s, KEY_CHUNK) for s in range(0, plen, KEY_CHUNK)] + [(plen, suf)]
+    per_step = HEADS_PER_STEP
+    group = units * width // (heads * HD)
+    steps = group // per_step
+    steps_per_unit = width // (per_step * HD)
+    units_per_head = units // heads
+
+    def attend(h, carry):
+        swap_copy(h).wait_recv()
+        k_buf[0:plen, :] = jnp.where(side == 0, got[h], other[h])
+        v_buf[0:plen, 0:HD] = jnp.where(side == 0, other[h], got[h])
+        cols = pl.ds(pl.multiple_of(h * HD, HD), HD)
+        k_buf[plen:, :] = suf_ref[0, :, cols]
+        v_buf[plen:, 0:HD] = suf_ref[1, :, cols]
+
+        def step(i, inner):
+            @pl.when((i == steps - 1) & (h + 1 < heads))
+            def _():
+                prepare(h + 1)
+
+            unit = h * units_per_head + i // steps_per_unit
+            for j in range(per_step):
+                start_col = (h * group + i * per_step + j) * HD
+                q = q_ref[:, pl.ds(pl.multiple_of(start_col, HD), HD)]
+                scores = []
+                for start, size in chunks:
+                    s = lax.dot_general(
+                        q, k_buf[start : start + size, :], (((1,), (1,)), ((), ())),
+                        preferred_element_type=jnp.float32,
+                    )
+                    if start == plen:
+                        s = s + bias_buf[...]
+                    scores.append(s)
+                top = functools.reduce(jnp.maximum, [jnp.max(s, axis=1, keepdims=True) for s in scores])
+                shift = top * scale
+                total = None
+                for (start, size), s in zip(chunks, scores):
+                    p = jnp.exp2(s * scale - shift).astype(jnp.bfloat16)
+                    part = jnp.dot(p, v_buf[start : start + size, :], preferred_element_type=jnp.float32)
+                    total = part if total is None else total + part
+                place = (i % steps_per_unit) * per_step * HD + j * HD
+                att[z, unit, :, pl.ds(pl.multiple_of(place, HD), HD)] = (total[:, 0:HD] / total[:, HD:]).astype(
+                    jnp.bfloat16
+                )
+
+            @pl.when(i % steps_per_unit == steps_per_unit - 1)
+            def _():
+                pieces(unit)
+
+            return inner
+
+        lax.fori_loop(0, steps, step, 0)
+        return carry
+
+    lax.fori_loop(0, heads, attend, 0)
+
+    def finish(u, carry):
+        pieces(u)
+        return carry
+
+    lax.fori_loop(units, units + prompts - 1, finish, 0)
+
+    col_count = y_send.shape[2]
+    theirs = pl.ds(pl.multiple_of((1 - here) * col_count, col_count), col_count)
+    ours = pl.ds(pl.multiple_of(here * col_count, col_count), col_count)
+
+    def y_copy(p):
+        return remote(y_send.at[p], y_recv.at[p], y_send_sem.at[p], y_recv_sem.at[p], beside)
+
+    def give(p, carry):
+        y_send[p] = acc[p, :, theirs].astype(jnp.bfloat16)
+        y_copy(p).start()
+        return carry
+
+    def take(p, carry):
+        y_copy(p).wait()
+        out_ref[p] = (acc[p, :, ours] + y_recv[p].astype(jnp.float32)).astype(jnp.bfloat16)
+        return carry
+
+    lax.fori_loop(0, prompts, give, 0)
+    lax.fori_loop(0, prompts, take, 0)
+
+    for h in range(heads):
+        core_copy(h).wait_send()
+        x_copy(h).wait_send()
+        swap_copy(h).wait_send()
+
+    def drain(u, carry):
+        for p in range(prompts):
+            @pl.when(has_left & (z <= p))
+            def _():
+                left_copy(p, u).wait_send()
+
+            @pl.when(has_right & (z >= p))
+            def _():
+                right_copy(p, u).wait_send()
+
+        return carry
+
+    lax.fori_loop(0, units, drain, 0)
+
+
+def fused(owner_index, suffix_lengths, queries, suffix_kv, prompt_cache, out_weight):
+    prompts = lax.axis_size("prompt")
+    rows, features = queries.shape[1:]
+    plen = prompt_cache.shape[3]
+    heads = prompt_cache.shape[4] // HD
+    suf = suffix_kv.shape[2]
+    units = 2 * heads
+    width = features // units
+    columns = out_weight.shape[1]
+    col_count = columns // 2
+    keys = plen + suf
+    half = pltpu.VMEM((heads, plen, HD), jnp.bfloat16)
+    dma = pltpu.SemaphoreType.DMA
+    vmem = pl.BlockSpec(memory_space=pltpu.VMEM)
+    smem = pl.BlockSpec(memory_space=pltpu.SMEM)
+    hbm = pl.BlockSpec(memory_space=pl.ANY)
+    return pl.pallas_call(
+        fused_kernel,
+        out_shape=jax.ShapeDtypeStruct((prompts, rows, col_count), jnp.bfloat16),
+        in_specs=[smem, smem, vmem, vmem, hbm, hbm],
+        out_specs=vmem,
+        scratch_shapes=[
+            half, half, half, half,
+            pltpu.VMEM((keys, HD), jnp.bfloat16),
+            pltpu.VMEM((keys, 2 * HD), jnp.bfloat16),
+            pltpu.VMEM((suf, suf), jnp.float32),
+            pltpu.VMEM((prompts, units, rows, width), jnp.bfloat16),
+            pltpu.VMEM((features, columns), jnp.bfloat16),
+            pltpu.VMEM((prompts, rows, columns), jnp.float32),
+            pltpu.VMEM((prompts, rows, col_count), jnp.bfloat16),
+            pltpu.VMEM((prompts, rows, col_count), jnp.bfloat16),
+            dma((heads,)), dma((heads,)), dma((heads,)), dma((heads,)), dma((heads,)), dma((heads,)), dma((heads,)),
+            dma((prompts, units)), dma((prompts, units)), dma((prompts, units)),
+            dma((prompts,)), dma((prompts,)), dma,
+        ],
+        compiler_params=pltpu.CompilerParams(
+            collective_id=0, has_side_effects=True, vmem_limit_bytes=60 * 1024 * 1024
+        ),
+        cost_estimate=pl.CostEstimate(
+            flops=4 * rows * features * keys + 2 * prompts * rows * features * columns,
+            bytes_accessed=4 * plen * heads * HD + 2 * features * columns,
+            transcendentals=rows * (features // HD) * keys,
+        ),
+    )(
+        owner_index, suffix_lengths.reshape(1), queries[0], suffix_kv[:, 0], prompt_cache[:, 0, 0], out_weight
+    )
+
+
 def body(owner_index, suffix_lengths, queries, suffix_kv, prompt_cache, out_weight):
     cand_count = lax.axis_size("cand")
     prompt_count = lax.axis_size("prompt")
     tensor_count = lax.axis_size("tensor")
+    if (cand_count, prompt_count, tensor_count) == (4, 4, 2):
+        return fused(owner_index, suffix_lengths, queries, suffix_kv, prompt_cache, out_weight)
     owner = owner_index[0]
     me = lax.axis_index("cand")
     side = me % 2

time: 305 us -> 225 us (0.74)
  waiting for transfers between devices: 146 us -> 0 us
  Pallas kernels: 87.2 us -> 221 us
  matrix products: 26.8 us -> 0 us
  between operations: 14.6 us -> 1.3 us
  other arithmetic: 12.1 us -> 0 us
  local copies, waits for them, and re-layouts: 10.5 us -> 2.26 us
  starting transfers between devices: 8.01 us -> 0 us
    pallas_call x4 -> x1, Pallas kernels: 87.2 us -> 221 us  [fused(): pl.pallas_call(fused_kernel, out_shape=jax.ShapeDtypeStruct((prompts, row...]
    all_gather x4 -> x0, waiting for transfers between devices: 91.1 us -> none  [body(): gathered.append(lax.all_gather(done, 'prompt', axis=0, tiled=True))]
    ppermute x13 -> x0, waiting for transfers between devices: 54.4 us -> none  [the longest x4 28.4 us: body(): got = lax.ppermute(part, 'cand', flip_perm(cand_count, bit))]
    dot_general x8 -> x0, matrix products: 26.8 us -> none  [project(): part = jnp.dot(gathered[head], piece, preferred_element_type=jnp.float32)]
    select_n x5 -> x0, other arithmetic: 10 us -> none  [the longest x4 5.35 us: body(): part = jnp.where(same(bit), part, got)]
    ppermute x13 -> x0, starting transfers between devices: 7.48 us -> none  [the longest x4 4.63 us: body(): got = lax.ppermute(part, 'cand', flip_perm(cand_count, bit))]
    squeeze x2 -> x0, local copies, waits for them, and re-layouts: 7.03 us -> none  [the longest x1 5.96 us: body(): keep = lax.dynamic_index_in_dim(cache, side, 0, keepdims=False)]
  transfers between devices with their start and end apart: 17 -> 0, of which waited for: 15 -> 0; matrix products, arithmetic and copies ran while one was open for 9% -> 0% of each run, Pallas kernels for 29% -> 0%
where the time goes in v2:
time: 225 us
  Pallas kernels  221 us (98%)
  local copies, waits for them, and re-layouts  2.26 us (1%)
    pallas_call x1, Pallas kernels, fused(): pl.pallas_call(fused_kernel, out_shape=jax.ShapeDtypeStruct((prompts, row...  221 us

profile of v2, /device:TPU:0, one launch (start us, length us, event | category | flops | bytes accessed | tf_op | source)
XLA Modules:
  0.0 224.6 jit_solution(6265232968515812757)
XLA Ops:
  1.3 221.1 %shard_map.64 = bf16[4,256,512]{2,1,0:T(8,128)(2,1)} custom-call(s32[1]{0:T(128)S(6)} %copy.8.owner_ref, s32[1]{0:T(128)} %bitcast.4.length_ref, bf16[256,4096]{1,0:T(8,128)(2,1)} %bitcast.6, bf16[2,256,512]{2,1,0:T(8,128)(2,1)} %bitcast.7, bf16[2,4096,512]{2,1,0:T(8,128)(2,1)} %bitcast.5, bf16[4096,1024]{1,0:T(8,128)(2,1)} %w_ref.1), custom_call_target="tpu_custom_call" | custom-call | flops 26843545600 | bytes 16777216 | tf_op jit(solution)/shard_map/pallas_call | solution.py:370
  222.4 2.3 %copy.10 = bf16[4,256,512]{2,1,0:T(8,128)(2,1)} copy(bf16[4,256,512]{2,1,0:T(8,128)(2,1)} %shard_map.64) | data formatting | bytes 2097152

commit v3 on v2

--- a/solution.py
+++ b/solution.py
@@ -99,10 +99,13 @@
 
 
 def fused_kernel(
-    owner_ref, length_ref, q_ref, suf_ref, cache_ref, w_ref, out_ref,
+    owner_ref, length_ref, q_ref, suf_ref, cache_ref, w_ref, out_ref, near_ref,
     keep, got, xgot, other, k_buf, v_buf, bias_buf, att, w_buf, acc, y_send, y_recv,
+    near_buf, near_acc, near_send, near_recv, near_done, near_in,
     keep_sem, core_send, core_recv, x_send, x_recv, swap_send, swap_recv,
     left_send, right_send, z_recv, y_send_sem, y_recv_sem, w_sem,
+    near_z_send, near_z_recv, near_core_send, near_core_recv, near_sem,
+    near_y_send, near_y_recv, near_out_send, near_out_recv,
 ):
     heads, plen, _ = keep.shape
     prompts, units, rows, width = att.shape
@@ -162,6 +165,39 @@
     def w_copy():
         return pltpu.make_async_copy(w_ref, w_buf, w_sem)
 
+    inner = (z == 1) | (z == 2)
+    outer = (z == 0) | (z == prompts - 1)
+    inward = {"prompt": 1 + z // 3}
+    outward = {"prompt": (z - 1) * 3}
+
+    def unit_rows(u):
+        return pl.ds(pl.multiple_of(u * width, width), width)
+
+    def near_z_copy(j):
+        part = unit_rows(2 * j + side)
+        return remote(w_ref.at[part], near_ref.at[part], near_z_send.at[j], near_z_recv.at[j], inward)
+
+    def near_core_copy(j):
+        part = unit_rows(2 * j + side)
+        return remote(near_ref.at[part], near_ref.at[part], near_core_send.at[j], near_core_recv.at[j], core)
+
+    def near_load(j):
+        part = pl.ds(pl.multiple_of(2 * j * width, 2 * width), 2 * width)
+        return pltpu.make_async_copy(near_ref.at[part], near_buf, near_sem)
+
+    def near_y_copy():
+        return remote(near_send, near_recv, near_y_send, near_y_recv, beside)
+
+    def near_out_copy():
+        return remote(near_done, near_in, near_out_send, near_out_recv, outward)
+
+    def y_copy(p):
+        return remote(y_send.at[p], y_recv.at[p], y_send_sem.at[p], y_recv_sem.at[p], beside)
+
+    col_count = y_send.shape[2]
+    theirs = pl.ds(pl.multiple_of((1 - here) * col_count, col_count), col_count)
+    ours = pl.ds(pl.multiple_of(here * col_count, col_count), col_count)
+
     owner = owner_ref[0]
     same_core = lax.rem(owner, 2) == side
     same_chip = lax.div(owner, 2) == lax.div(me, 2)
@@ -171,6 +207,11 @@
         keep_copy(h).start()
     w_copy().start()
 
+    @pl.when(outer)
+    def _():
+        for j in range(units // 2):
+            near_z_copy(j).start()
+
     v_buf[:, HD:] = jnp.ones((plen + suf, HD), jnp.bfloat16)
     row = lax.broadcasted_iota(jnp.int32, (suf, suf), 0)
     col = lax.broadcasted_iota(jnp.int32, (suf, suf), 1)
@@ -201,34 +242,76 @@
 
     prepare(0)
     acc[...] = jnp.zeros_like(acc)
+    near_acc[...] = jnp.zeros_like(near_acc)
     w_copy().wait()
 
     def in_range(u):
         return (u >= 0) & (u < units)
 
-    def project(u):
-        def block(p, carry):
-            acc[p] += jnp.dot(
-                att[p, u], w_buf[pl.ds(pl.multiple_of(u * width, width), width), :],
-                preferred_element_type=jnp.float32,
-            )
-            return carry
-
-        lax.fori_loop(0, prompts, block, 0)
+    def project(p, u):
+        acc[p] += jnp.dot(att[p, u], w_buf[unit_rows(u), :], preferred_element_type=jnp.float32)
+
+        @pl.when(u == units - 1)
+        def _():
+            y_send[p] = acc[p, :, theirs].astype(jnp.bfloat16)
+            y_copy(p).start()
+
+    def lend(u):
+        @pl.when(inner & (u == units // 2))
+        def _():
+            for j in range(units // 2):
+                near_z_copy(j).wait_recv()
+                near_core_copy(j).start()
+
+        @pl.when(inner & (u > units // 2) & (u < units))
+        def _():
+            low = u - units // 2 - 1
+
+            def pair(j, carry):
+                near_core_copy(j).wait_recv()
+                near_load(j).start()
+                near_load(j).wait()
+                for k in range(2):
+                    near_acc[...] += jnp.dot(
+                        att[z, 2 * j + k], near_buf[k * width : (k + 1) * width, :],
+                        preferred_element_type=jnp.float32,
+                    )
+                return carry
+
+            lax.fori_loop(low, jnp.where(u == units - 1, units // 2, low + 1), pair, 0)
+
+        @pl.when(inner & (u == units - 1))
+        def _():
+            near_send[...] = near_acc[:, theirs].astype(jnp.bfloat16)
+            near_y_copy().start()
+
+        @pl.when(inner & (u == units))
+        def _():
+            near_y_copy().wait()
+            near_done[...] = (near_acc[:, ours] + near_recv[...].astype(jnp.float32)).astype(jnp.bfloat16)
+            near_out_copy().start()
 
     def pieces(u):
-        @pl.when((u < units) & has_left)
+        @pl.when((u < units) & has_left & (z != 1))
         def _():
             left_copy(z, u).start()
 
-        @pl.when((u < units) & has_right)
+        @pl.when((u < units) & has_right & (z != prompts - 2))
         def _():
             right_copy(z, u).start()
+
+        lend(u)
+
+        @pl.when(u < units)
+        def _():
+            project(z, u)
 
         for hop in range(1, prompts):
             late = u - hop
-
-            @pl.when(in_range(late) & (z >= hop))
+            from_left = (z >= hop) if hop > 1 else inner
+            from_right = (z + hop < prompts) if hop > 1 else inner
+
+            @pl.when(in_range(late) & from_left)
             def _():
                 right_copy(z - hop, late).wait_recv()
 
@@ -236,7 +319,7 @@
                 def _():
                     right_copy(z - hop, late).start()
 
-            @pl.when(in_range(late) & (z + hop < prompts))
+            @pl.when(in_range(late) & from_right)
             def _():
                 left_copy(z + hop, late).wait_recv()
 
@@ -244,9 +327,13 @@
                 def _():
                     left_copy(z + hop, late).start()
 
-        @pl.when(in_range(u - prompts + 1))
-        def _():
-            project(u - prompts + 1)
+            @pl.when(in_range(late) & from_left)
+            def _():
+                project(z - hop, late)
+
+            @pl.when(in_range(late) & from_right)
+            def _():
+                project(z + hop, late)
 
     scale = math.log2(math.e) / math.sqrt(HD)
     chunks = [(s, KEY_CHUNK) for s in range(0, plen, KEY_CHUNK)] + [(plen, suf)]
@@ -270,29 +357,30 @@
                 prepare(h + 1)
 
             unit = h * units_per_head + i // steps_per_unit
+            start_col = (h * group + i * per_step) * HD
+            q = jnp.concatenate(
+                [q_ref[:, pl.ds(pl.multiple_of(start_col + j * HD, HD), HD)] for j in range(per_step)], axis=0
+            )
+            scores = []
+            for start, size in chunks:
+                s = lax.dot_general(
+                    q, k_buf[start : start + size, :], (((1,), (1,)), ((), ())),
+                    preferred_element_type=jnp.float32,
+                )
+                if start == plen:
+                    s = s + jnp.concatenate([bias_buf[...]] * per_step, axis=0)
+                scores.append(s)
+            top = functools.reduce(jnp.maximum, [jnp.max(s, axis=1, keepdims=True) for s in scores])
+            shift = top * scale
+            total = None
+            for (start, size), s in zip(chunks, scores):
+                p = jnp.exp2(s * scale - shift).astype(jnp.bfloat16)
+                part = jnp.dot(p, v_buf[start : start + size, :], preferred_element_type=jnp.float32)
+                total = part if total is None else total + part
+            place = (i % steps_per_unit) * per_step * HD
+            done = (total[:, 0:HD] / total[:, HD:]).astype(jnp.bfloat16)
             for j in range(per_step):
-                start_col = (h * group + i * per_step + j) * HD
-                q = q_ref[:, pl.ds(pl.multiple_of(start_col, HD), HD)]
-                scores = []
-                for start, size in chunks:
-                    s = lax.dot_general(
-                        q, k_buf[start : start + size, :], (((1,), (1,)), ((), ())),
-                        preferred_element_type=jnp.float32,
-                    )
-                    if start == plen:
-                        s = s + bias_buf[...]
-                    scores.append(s)
-                top = functools.reduce(jnp.maximum, [jnp.max(s, axis=1, keepdims=True) for s in scores])
-                shift = top * scale
-                total = None
-                for (start, size), s in zip(chunks, scores):
-                    p = jnp.exp2(s * scale - shift).astype(jnp.bfloat16)
-                    part = jnp.dot(p, v_buf[start : start + size, :], preferred_element_type=jnp.float32)
-                    total = part if total is None else total + part
-                place = (i % steps_per_unit) * per_step * HD + j * HD
-                att[z, unit, :, pl.ds(pl.multiple_of(place, HD), HD)] = (total[:, 0:HD] / total[:, HD:]).astype(
-                    jnp.bfloat16
-                )
+                att[z, unit, :, pl.ds(pl.multiple_of(place + j * HD, HD), HD)] = done[j * rows : (j + 1) * rows]
 
             @pl.when(i % steps_per_unit == steps_per_unit - 1)
             def _():
@@ -311,38 +399,42 @@
 
     lax.fori_loop(units, units + prompts - 1, finish, 0)
 
-    col_count = y_send.shape[2]
-    theirs = pl.ds(pl.multiple_of((1 - here) * col_count, col_count), col_count)
-    ours = pl.ds(pl.multiple_of(here * col_count, col_count), col_count)
-
-    def y_copy(p):
-        return remote(y_send.at[p], y_recv.at[p], y_send_sem.at[p], y_recv_sem.at[p], beside)
-
-    def give(p, carry):
-        y_send[p] = acc[p, :, theirs].astype(jnp.bfloat16)
-        y_copy(p).start()
-        return carry
-
-    def take(p, carry):
-        y_copy(p).wait()
-        out_ref[p] = (acc[p, :, ours] + y_recv[p].astype(jnp.float32)).astype(jnp.bfloat16)
-        return carry
-
-    lax.fori_loop(0, prompts, give, 0)
-    lax.fori_loop(0, prompts, take, 0)
+    for p in range(prompts):
+        borrowed = outer & (p == 1 + z // 3)
+
+        @pl.when(jnp.logical_not(borrowed))
+        def _():
+            y_copy(p).wait()
+            out_ref[p] = (acc[p, :, ours] + y_recv[p].astype(jnp.float32)).astype(jnp.bfloat16)
+
+        @pl.when(borrowed)
+        def _():
+            near_out_copy().wait_recv()
+            out_ref[p] = near_in[...]
 
     for h in range(heads):
         core_copy(h).wait_send()
         x_copy(h).wait_send()
         swap_copy(h).wait_send()
 
+    @pl.when(outer)
+    def _():
+        for j in range(units // 2):
+            near_z_copy(j).wait_send()
+
+    @pl.when(inner)
+    def _():
+        for j in range(units // 2):
+            near_core_copy(j).wait_send()
+        near_out_copy().wait_send()
+
     def drain(u, carry):
         for p in range(prompts):
-            @pl.when(has_left & (z <= p))
+            @pl.when(has_left & ((z < p) | (z == p) & (z != 1)))
             def _():
                 left_copy(p, u).wait_send()
 
-            @pl.when(has_right & (z >= p))
+            @pl.when(has_right & ((z > p) | (z == p) & (z != prompts - 2)))
             def _():
                 right_copy(p, u).wait_send()
 
@@ -363,15 +455,19 @@
     col_count = columns // 2
     keys = plen + suf
     half = pltpu.VMEM((heads, plen, HD), jnp.bfloat16)
+    block = pltpu.VMEM((rows, col_count), jnp.bfloat16)
     dma = pltpu.SemaphoreType.DMA
     vmem = pl.BlockSpec(memory_space=pltpu.VMEM)
     smem = pl.BlockSpec(memory_space=pltpu.SMEM)
     hbm = pl.BlockSpec(memory_space=pl.ANY)
     return pl.pallas_call(
         fused_kernel,
-        out_shape=jax.ShapeDtypeStruct((prompts, rows, col_count), jnp.bfloat16),
+        out_shape=[
+            jax.ShapeDtypeStruct((prompts, rows, col_count), jnp.bfloat16),
+            jax.ShapeDtypeStruct((features, columns), jnp.bfloat16),
+        ],
         in_specs=[smem, smem, vmem, vmem, hbm, hbm],
-        out_specs=vmem,
+        out_specs=[vmem, hbm],
         scratch_shapes=[
             half, half, half, half,
             pltpu.VMEM((keys, HD), jnp.bfloat16),
@@ -382,12 +478,16 @@
             pltpu.VMEM((prompts, rows, columns), jnp.float32),
             pltpu.VMEM((prompts, rows, col_count), jnp.bfloat16),
             pltpu.VMEM((prompts, rows, col_count), jnp.bfloat16),
+            pltpu.VMEM((2 * width, columns), jnp.bfloat16),
+            pltpu.VMEM((rows, columns), jnp.float32),
+            block, block, block, block,
             dma((heads,)), dma((heads,)), dma((heads,)), dma((heads,)), dma((heads,)), dma((heads,)), dma((heads,)),
             dma((prompts, units)), dma((prompts, units)), dma((prompts, units)),
             dma((prompts,)), dma((prompts,)), dma,
+            dma((units // 2,)), dma((units // 2,)), dma((units // 2,)), dma((units // 2,)), dma, dma, dma, dma, dma,
         ],
         compiler_params=pltpu.CompilerParams(
-            collective_id=0, has_side_effects=True, vmem_limit_bytes=60 * 1024 * 1024
+            collective_id=0, has_side_effects=True, vmem_limit_bytes=62 * 1024 * 1024
         ),
         cost_estimate=pl.CostEstimate(
             flops=4 * rows * features * keys + 2 * prompts * rows * features * columns,
@@ -396,7 +496,7 @@
         ),
     )(
         owner_index, suffix_lengths.reshape(1), queries[0], suffix_kv[:, 0], prompt_cache[:, 0, 0], out_weight
-    )
+    )[0]
 
 
 def body(owner_index, suffix_lengths, queries, suffix_kv, prompt_cache, out_weight):

time: 225 us -> 247 us (1.098)
  Pallas kernels: 221 us -> 243 us
    pallas_call x1, Pallas kernels: 221 us -> 243 us  [fused(): pl.pallas_call(fused_kernel, out_shape=[jax.ShapeDtypeStruct((prompts, ro...]
where the time goes in v3:
time: 247 us
  Pallas kernels  243 us (98%)
    pallas_call x1, Pallas kernels, fused(): pl.pallas_call(fused_kernel, out_shape=[jax.ShapeDtypeStruct((prompts, ro...  243 us

profile of v3, /device:TPU:0, one launch (start us, length us, event | category | flops | bytes accessed | tf_op | source)
XLA Modules:
  0.0 247.0 jit_solution(15900894866662519375)
XLA Ops:
  1.3 243.4 %shard_map.64 = (bf16[4,256,512]{2,1,0:T(8,128)(2,1)}, bf16[4096,1024]{1,0:T(8,128)(2,1)}) custom-call(s32[1]{0:T(128)S(6)} %copy.8.owner_ref, s32[1]{0:T(128)} %bitcast.4.length_ref, bf16[256,4096]{1,0:T(8,128)(2,1)} %bitcast.6, bf16[2,256,512]{2,1,0:T(8,128)(2,1)} %bitcast.7, bf16[2,4096,512]{2,1,0:T(8,128)(2,1)} %bitcast.5, bf16[4096,1024]{1,0:T(8,128)(2,1)} %w_ref.1), custom_call_target="tpu_custom_call" | custom-call | flops 26843545600 | bytes 16777216 | tf_op jit(solution)/shard_map/pallas_call | solution.py:463
  244.7 2.3 copy.10

commit v4 on v3

--- a/solution.py
+++ b/solution.py
@@ -357,30 +357,29 @@
                 prepare(h + 1)
 
             unit = h * units_per_head + i // steps_per_unit
-            start_col = (h * group + i * per_step) * HD
-            q = jnp.concatenate(
-                [q_ref[:, pl.ds(pl.multiple_of(start_col + j * HD, HD), HD)] for j in range(per_step)], axis=0
-            )
-            scores = []
-            for start, size in chunks:
-                s = lax.dot_general(
-                    q, k_buf[start : start + size, :], (((1,), (1,)), ((), ())),
-                    preferred_element_type=jnp.float32,
+            for j in range(per_step):
+                start_col = (h * group + i * per_step + j) * HD
+                q = q_ref[:, pl.ds(pl.multiple_of(start_col, HD), HD)]
+                scores = []
+                for start, size in chunks:
+                    s = lax.dot_general(
+                        q, k_buf[start : start + size, :], (((1,), (1,)), ((), ())),
+                        preferred_element_type=jnp.float32,
+                    )
+                    if start == plen:
+                        s = s + bias_buf[...]
+                    scores.append(s)
+                top = functools.reduce(jnp.maximum, [jnp.max(s, axis=1, keepdims=True) for s in scores])
+                shift = top * scale
+                total = None
+                for (start, size), s in zip(chunks, scores):
+                    p = jnp.exp2(s * scale - shift).astype(jnp.bfloat16)
+                    part = jnp.dot(p, v_buf[start : start + size, :], preferred_element_type=jnp.float32)
+                    total = part if total is None else total + part
+                place = (i % steps_per_unit) * per_step * HD + j * HD
+                att[z, unit, :, pl.ds(pl.multiple_of(place, HD), HD)] = (total[:, 0:HD] / total[:, HD:]).astype(
+                    jnp.bfloat16
                 )
-                if start == plen:
-                    s = s + jnp.concatenate([bias_buf[...]] * per_step, axis=0)
-                scores.append(s)
-            top = functools.reduce(jnp.maximum, [jnp.max(s, axis=1, keepdims=True) for s in scores])
-            shift = top * scale
-            total = None
-            for (start, size), s in zip(chunks, scores):
-                p = jnp.exp2(s * scale - shift).astype(jnp.bfloat16)
-                part = jnp.dot(p, v_buf[start : start + size, :], preferred_element_type=jnp.float32)
-                total = part if total is None else total + part
-            place = (i % steps_per_unit) * per_step * HD
-            done = (total[:, 0:HD] / total[:, HD:]).astype(jnp.bfloat16)
-            for j in range(per_step):
-                att[z, unit, :, pl.ds(pl.multiple_of(place + j * HD, HD), HD)] = done[j * rows : (j + 1) * rows]
 
             @pl.when(i % steps_per_unit == steps_per_unit - 1)
             def _():

time: 247 us -> 234 us (0.947)
  Pallas kernels: 243 us -> 230 us
    pallas_call x1, Pallas kernels: 243 us -> 230 us  [fused(): pl.pallas_call(fused_kernel, out_shape=[jax.ShapeDtypeStruct((prompts, ro...]
where the time goes in v4:
time: 234 us
  Pallas kernels  230 us (98%)
    pallas_call x1, Pallas kernels, fused(): pl.pallas_call(fused_kernel, out_shape=[jax.ShapeDtypeStruct((prompts, ro...  230 us

profile of v4, /device:TPU:0, one launch (start us, length us, event | category | flops | bytes accessed | tf_op | source)
XLA Modules:
  0.0 233.5 jit_solution(10853287088611488007)
XLA Ops:
  1.3 229.9 %shard_map.64 = (bf16[4,256,512]{2,1,0:T(8,128)(2,1)}, bf16[4096,1024]{1,0:T(8,128)(2,1)}) custom-call(s32[1]{0:T(128)S(6)} %copy.8.owner_ref, s32[1]{0:T(128)} %bitcast.4.length_ref, bf16[256,4096]{1,0:T(8,128)(2,1)} %bitcast.6, bf16[2,256,512]{2,1,0:T(8,128)(2,1)} %bitcast.7, bf16[2,4096,512]{2,1,0:T(8,128)(2,1)} %bitcast.5, bf16[4096,1024]{1,0:T(8,128)(2,1)} %w_ref.1), custom_call_target="tpu_custom_call" | custom-call | flops 26843545600 | bytes 16777216 | tf_op jit(solution)/shard_map/pallas_call | solution.py:462
  231.2 2.3 copy.10

commit v5 on v3

--- a/solution.py
+++ b/solution.py
@@ -101,11 +101,11 @@
 def fused_kernel(
     owner_ref, length_ref, q_ref, suf_ref, cache_ref, w_ref, out_ref, near_ref,
     keep, got, xgot, other, k_buf, v_buf, bias_buf, att, w_buf, acc, y_send, y_recv,
-    near_buf, near_acc, near_send, near_recv, near_done, near_in,
+    near_buf, near_acc, near_send, near_recv, near_done, near_in, scores,
     keep_sem, core_send, core_recv, x_send, x_recv, swap_send, swap_recv,
     left_send, right_send, z_recv, y_send_sem, y_recv_sem, w_sem,
     near_z_send, near_z_recv, near_core_send, near_core_recv, near_sem,
-    near_y_send, near_y_recv, near_out_send, near_out_recv,
+    near_y_send, near_y_recv, near_out_send, near_out_recv, q_sem,
 ):
     heads, plen, _ = keep.shape
     prompts, units, rows, width = att.shape
@@ -162,6 +162,9 @@
     def right_copy(p, u):
         return remote(att.at[p, u], att.at[p, u], right_send.at[p, u], z_recv.at[p, u], right)
 
+    def q_copy(u):
+        return pltpu.make_async_copy(q_ref.at[:, pl.ds(u * width, width)], att.at[z, u], q_sem.at[u])
+
     def w_copy():
         return pltpu.make_async_copy(w_ref, w_buf, w_sem)
 
@@ -182,8 +185,7 @@
         return remote(near_ref.at[part], near_ref.at[part], near_core_send.at[j], near_core_recv.at[j], core)
 
     def near_load(j):
-        part = pl.ds(pl.multiple_of(2 * j * width, 2 * width), 2 * width)
-        return pltpu.make_async_copy(near_ref.at[part], near_buf, near_sem)
+        return pltpu.make_async_copy(near_ref.at[unit_rows(j)], near_buf, near_sem)
 
     def near_y_copy():
         return remote(near_send, near_recv, near_y_send, near_y_recv, beside)
@@ -205,17 +207,19 @@
     for h in range(heads):
         core_copy(h).start()
         keep_copy(h).start()
+    for u in range(units):
+        q_copy(u).start()
     w_copy().start()
 
     @pl.when(outer)
     def _():
-        for j in range(units // 2):
+        for j in range(units // 4):
             near_z_copy(j).start()
 
     v_buf[:, HD:] = jnp.ones((plen + suf, HD), jnp.bfloat16)
-    row = lax.broadcasted_iota(jnp.int32, (suf, suf), 0)
-    col = lax.broadcasted_iota(jnp.int32, (suf, suf), 1)
-    bias_buf[...] = jnp.where((col <= row) & (col < length_ref[0]), 0.0, -1e30)
+    row = lax.broadcasted_iota(jnp.int32, bias_buf.shape, 0)
+    col = lax.broadcasted_iota(jnp.int32, bias_buf.shape, 1) - (bias_buf.shape[1] - suf)
+    bias_buf[...] = jnp.where((col < 0) | (col <= row) & (col < length_ref[0]), 0.0, -1e30)
 
     def first(h, carry):
         keep_copy(h).wait()
@@ -244,6 +248,8 @@
     acc[...] = jnp.zeros_like(acc)
     near_acc[...] = jnp.zeros_like(near_acc)
     w_copy().wait()
+    for u in range(units):
+        q_copy(u).wait()
 
     def in_range(u):
         return (u >= 0) & (u < units)
@@ -257,35 +263,37 @@
             y_copy(p).start()
 
     def lend(u):
-        @pl.when(inner & (u == units // 2))
+        for j in range(units // 4, units // 2):
+            @pl.when(outer & (u == 2 * j - units // 2 + 1))
+            def _():
+                near_z_copy(j).start()
+
+        @pl.when(inner & (u == units - 2))
         def _():
             for j in range(units // 2):
                 near_z_copy(j).wait_recv()
                 near_core_copy(j).start()
 
-        @pl.when(inner & (u > units // 2) & (u < units))
-        def _():
-            low = u - units // 2 - 1
+        @pl.when(inner & ((u == units - 1) | (u == units)))
+        def _():
+            low = (u - units + 1) * (units // 4)
 
             def pair(j, carry):
                 near_core_copy(j).wait_recv()
-                near_load(j).start()
-                near_load(j).wait()
                 for k in range(2):
-                    near_acc[...] += jnp.dot(
-                        att[z, 2 * j + k], near_buf[k * width : (k + 1) * width, :],
-                        preferred_element_type=jnp.float32,
-                    )
+                    near_load(2 * j + k).start()
+                    near_load(2 * j + k).wait()
+                    near_acc[...] += jnp.dot(att[z, 2 * j + k], near_buf[...], preferred_element_type=jnp.float32)
                 return carry
 
-            lax.fori_loop(low, jnp.where(u == units - 1, units // 2, low + 1), pair, 0)
-
-        @pl.when(inner & (u == units - 1))
+            lax.fori_loop(low, low + units // 4, pair, 0)
+
+        @pl.when(inner & (u == units))
         def _():
             near_send[...] = near_acc[:, theirs].astype(jnp.bfloat16)
             near_y_copy().start()
 
-        @pl.when(inner & (u == units))
+        @pl.when(inner & (u == units + 1))
         def _():
             near_y_copy().wait()
             near_done[...] = (near_acc[:, ours] + near_recv[...].astype(jnp.float32)).astype(jnp.bfloat16)
@@ -307,7 +315,7 @@
             project(z, u)
 
         for hop in range(1, prompts):
-            late = u - hop
+            late = u - hop - 1
             from_left = (z >= hop) if hop > 1 else inner
             from_right = (z + hop < prompts) if hop > 1 else inner
 
@@ -336,12 +344,11 @@
                 project(z + hop, late)
 
     scale = math.log2(math.e) / math.sqrt(HD)
-    chunks = [(s, KEY_CHUNK) for s in range(0, plen, KEY_CHUNK)] + [(plen, suf)]
-    per_step = HEADS_PER_STEP
+    keys = plen + suf
+    starts = list(range(0, plen, KEY_CHUNK))
+    chunks = list(zip(starts, starts[1:] + [keys]))
     group = units * width // (heads * HD)
-    steps = group // per_step
-    steps_per_unit = width // (per_step * HD)
-    units_per_head = units // heads
+    per_unit = width // HD
 
     def attend(h, carry):
         swap_copy(h).wait_recv()
@@ -351,44 +358,65 @@
         k_buf[plen:, :] = suf_ref[0, :, cols]
         v_buf[plen:, 0:HD] = suf_ref[1, :, cols]
 
-        def step(i, inner):
-            @pl.when((i == steps - 1) & (h + 1 < heads))
+        def query(i):
+            place = (i % per_unit) * HD
+            return att[z, (h * group + i) // per_unit, :, pl.ds(pl.multiple_of(place, HD), HD)]
+
+        def score(q, slot, chunk, top):
+            start, end = chunk
+            s = lax.dot_general(
+                q, k_buf[start:end, :], (((1,), (1,)), ((), ())), preferred_element_type=jnp.float32
+            )
+            if end == keys:
+                s = s + bias_buf[...]
+            scores[slot, :, start:end] = s
+            high = jnp.max(s, axis=1, keepdims=True)
+            return high if top is None else jnp.maximum(top, high)
+
+        def weigh(slot, chunk, shift, total):
+            start, end = chunk
+            p = jnp.exp2(scores[slot, :, start:end] * scale - shift).astype(jnp.bfloat16)
+            part = jnp.dot(p, v_buf[start:end, :], preferred_element_type=jnp.float32)
+            return part if total is None else total + part
+
+        def store(i, total):
+            unit = (h * group + i) // per_unit
+            place = (i % per_unit) * HD
+            att[z, unit, :, pl.ds(pl.multiple_of(place, HD), HD)] = (total[:, 0:HD] / total[:, HD:]).astype(
+                jnp.bfloat16
+            )
+
+            @pl.when(i % per_unit == per_unit - 1)
+            def _():
+                pieces(unit)
+
+        first_query = query(0)
+        top = None
+        for chunk in chunks:
+            top = score(first_query, 0, chunk, top)
+
+        def step(i, top):
+            @pl.when((i == group - 3) & (h + 1 < heads))
             def _():
                 prepare(h + 1)
 
-            unit = h * units_per_head + i // steps_per_unit
-            start_col = (h * group + i * per_step) * HD
-            q = jnp.concatenate(
-                [q_ref[:, pl.ds(pl.multiple_of(start_col + j * HD, HD), HD)] for j in range(per_step)], axis=0
-            )
-            scores = []
-            for start, size in chunks:
-                s = lax.dot_general(
-                    q, k_buf[start : start + size, :], (((1,), (1,)), ((), ())),
-                    preferred_element_type=jnp.float32,
-                )
-                if start == plen:
-                    s = s + jnp.concatenate([bias_buf[...]] * per_step, axis=0)
-                scores.append(s)
-            top = functools.reduce(jnp.maximum, [jnp.max(s, axis=1, keepdims=True) for s in scores])
             shift = top * scale
+            slot = lax.rem(i, 2)
+            q = query(i + 1)
+            later = None
             total = None
-            for (start, size), s in zip(chunks, scores):
-                p = jnp.exp2(s * scale - shift).astype(jnp.bfloat16)
-                part = jnp.dot(p, v_buf[start : start + size, :], preferred_element_type=jnp.float32)
-                total = part if total is None else total + part
-            place = (i % steps_per_unit) * per_step * HD
-            done = (total[:, 0:HD] / total[:, HD:]).astype(jnp.bfloat16)
-            for j in range(per_step):
-                att[z, unit, :, pl.ds(pl.multiple_of(place + j * HD, HD), HD)] = done[j * rows : (j + 1) * rows]
-
-            @pl.when(i % steps_per_unit == steps_per_unit - 1)
-            def _():
-                pieces(unit)
-
-            return inner
-
-        lax.fori_loop(0, steps, step, 0)
+            for chunk in chunks:
+                later = score(q, 1 - slot, chunk, later)
+                total = weigh(slot, chunk, shift, total)
+            store(i, total)
+            return later
+
+        top = lax.fori_loop(0, group - 1, step, top)
+        shift = top * scale
+        total = None
+        for chunk in chunks:
+            total = weigh((group - 1) % 2, chunk, shift, total)
+        store(jnp.int32(group - 1), total)
         return carry
 
     lax.fori_loop(0, heads, attend, 0)
@@ -397,7 +425,7 @@
         pieces(u)
         return carry
 
-    lax.fori_loop(units, units + prompts - 1, finish, 0)
+    lax.fori_loop(units, units + prompts, finish, 0)
 
     for p in range(prompts):
         borrowed = outer & (p == 1 + z // 3)
@@ -466,25 +494,27 @@
             jax.ShapeDtypeStruct((prompts, rows, col_count), jnp.bfloat16),
             jax.ShapeDtypeStruct((features, columns), jnp.bfloat16),
         ],
-        in_specs=[smem, smem, vmem, vmem, hbm, hbm],
+        in_specs=[smem, smem, hbm, vmem, hbm, hbm],
         out_specs=[vmem, hbm],
         scratch_shapes=[
             half, half, half, half,
             pltpu.VMEM((keys, HD), jnp.bfloat16),
             pltpu.VMEM((keys, 2 * HD), jnp.bfloat16),
-            pltpu.VMEM((suf, suf), jnp.float32),
+            pltpu.VMEM((rows, KEY_CHUNK + suf), jnp.float32),
             pltpu.VMEM((prompts, units, rows, width), jnp.bfloat16),
             pltpu.VMEM((features, columns), jnp.bfloat16),
             pltpu.VMEM((prompts, rows, columns), jnp.float32),
             pltpu.VMEM((prompts, rows, col_count), jnp.bfloat16),
             pltpu.VMEM((prompts, rows, col_count), jnp.bfloat16),
-            pltpu.VMEM((2 * width, columns), jnp.bfloat16),
+            pltpu.VMEM((width, columns), jnp.bfloat16),
             pltpu.VMEM((rows, columns), jnp.float32),
             block, block, block, block,
+            pltpu.VMEM((2, rows, keys), jnp.float32),
             dma((heads,)), dma((heads,)), dma((heads,)), dma((heads,)), dma((heads,)), dma((heads,)), dma((heads,)),
             dma((prompts, units)), dma((prompts, units)), dma((prompts, units)),
             dma((prompts,)), dma((prompts,)), dma,
             dma((units // 2,)), dma((units // 2,)), dma((units // 2,)), dma((units // 2,)), dma, dma, dma, dma, dma,
+            dma((units,)),
         ],
         compiler_params=pltpu.CompilerParams(
             collective_id=0, has_side_effects=True, vmem_limit_bytes=62 * 1024 * 1024

time: 247 us -> 210 us (0.85)
  Pallas kernels: 243 us -> 206 us
    pallas_call x1, Pallas kernels: 243 us -> 206 us  [fused(): pl.pallas_call(fused_kernel, out_shape=[jax.ShapeDtypeStruct((prompts, ro...]
where the time goes in v5:
time: 210 us; the launch traced here: 209 us
  Pallas kernels  206 us (98%)
  local copies, waits for them, and re-layouts  2.26 us (1%)
    pallas_call x1, Pallas kernels, fused(): pl.pallas_call(fused_kernel, out_shape=[jax.ShapeDtypeStruct((prompts, ro...  206 us

profile of v5, /device:TPU:0, one launch (start us, length us, event | category | flops | bytes accessed | tf_op | source)
XLA Modules:
  0.0 209.3 jit_solution(8376093810453415996)
XLA Ops:
  1.3 205.7 %shard_map.64 = (bf16[4,256,512]{2,1,0:T(8,128)(2,1)}, bf16[4096,1024]{1,0:T(8,128)(2,1)}) custom-call(s32[1]{0:T(128)S(6)} %copy.8.owner_ref, s32[1]{0:T(128)} %bitcast.4.length_ref, bf16[256,4096]{1,0:T(8,128)(2,1)} %bitcast.6, bf16[2,256,512]{2,1,0:T(8,128)(2,1)} %bitcast.7, bf16[2,4096,512]{2,1,0:T(8,128)(2,1)} %bitcast.5, bf16[4096,1024]{1,0:T(8,128)(2,1)} %w_ref.1), custom_call_target="tpu_custom_call" | custom-call | flops 26843545600 | bytes 16777216 | tf_op jit(solution)/shard_map/pallas_call | solution.py:491
  207.0 2.3 %copy.10 = bf16[4,256,512]{2,1,0:T(8,128)(2,1)} copy(bf16[4,256,512]{2,1,0:T(8,128)(2,1)} %get-tuple-element.6) | data formatting | bytes 2097152
